TPU v7x, 32 devices: a whole 2x2x4 slice. The times are simulated.
32 devices in a mesh: groups: 2 (over y), section: 4 (over z), fsdp: 4 (over x, core).
Axes of the slice: x: 2, y: 2, z: 4, core: 2. Of those that a mesh axis runs over, the one named last changes fastest.
Arguments:
- sent_act: bfloat16 [4, 1024, 4096], P('section', 'groups', 'fsdp'), parts along dimension 1, may hold values from -6 to 6
- sent_grad: bfloat16 [4, 1024, 4096], P('section', 'groups', 'fsdp'), parts along dimension 1, may hold values from -6 to 6
- stash_in: bfloat16 [4, 2, 1024, 4096], P('section', None, 'groups', 'fsdp'), parts along dimension 2, may hold values from -6 to 6
- stash_pre: bfloat16 [4, 2, 1024, 4096], P('section', None, 'groups', 'fsdp'), parts along dimension 2, may hold values from -6 to 6
- layer_weight: bfloat16 [4, 4096, 4096], P('section', None, 'fsdp'), may hold values from -0.125 to 0.125
- layer_bias: float32 [4, 4096], P('section', 'fsdp'), may hold values from -3 to 3
- seg_table: bfloat16 [4784, 4096], P('section', 'fsdp'), may hold values from -6 to 6
- seg_index: int32 [1024, 32], P('groups'), parts along dimension 0, may hold values from 0 to 4783
- seg_amp: float32 [1024, 32], P('groups'), parts along dimension 0, may hold values from -1.2 to 1.2
- field_angle: float32 [1024, 2], P('groups'), parts along dimension 0, may hold values from -1 to 1
- angle_weight: float32 [2, 4096], P(None, 'fsdp'), may hold values from -3 to 3
- target: bfloat16 [1024, 4096], P('groups', 'fsdp'), parts along dimension 0, may hold values from -6 to 6
- sched: int32 [4], P('section'), may hold values from 0 to 1
Outputs:
- fwd_out: bfloat16 [4, 1024, 4096], P('section', 'groups', 'fsdp'), parts along dimension 1
- grad_in: bfloat16 [4, 1024, 4096], P('section', 'groups', 'fsdp'), parts along dimension 1
- grad_w: bfloat16 [4, 8192, 4096], P('section', 'groups', 'fsdp'), parts along dimension 1
- grad_bias: float32 [4, 8192], P('section', ('groups', 'fsdp')), parts along dimension 1
There are 2 independent parts, one for each index of `groups`. A program takes and returns all parts, laid end to end along the dimension named above; an argument that names none is the same for every part. Nothing has to cross between parts.
All inputs are finite; a program needn't handle non-finite values.
Results may differ from a plain program's by a relative error of at most 0.017.
Values may be sent and summed in bfloat16 or wider, within the bound.
A program may use at most 128 MiB of HBM per device.

v0:
```python
import jax
import jax.numpy as jnp
from jax import lax
from jax.sharding import PartitionSpec as P


def from_behind(shard, axis, by):
    length = lax.axis_size(axis)
    pairs = [(i, i + by) for i in range(length) if 0 <= i + by < length]
    return lax.ppermute(shard, axis, pairs)


def lookup_sum(full_table, seg_index, seg_amp, first_row):
    row_count = full_table.shape[0]
    feature_count = full_table.shape[1]
    block_rows = 512
    block_count = (row_count + block_rows - 1) // block_rows
    padded = jnp.pad(full_table, ((0, block_count * block_rows - row_count), (0, 0)))
    blocks = padded.reshape(block_count, block_rows, feature_count)
    starts = jnp.arange(block_count, dtype=jnp.int32) * block_rows
    local_row = seg_index - first_row

    def add_block(total, item):
        table_block, start = item
        position = start + jnp.arange(block_rows, dtype=jnp.int32)
        matched = local_row[:, :, None] == position[None, None, :]
        amplitude = jnp.sum(jnp.where(matched, seg_amp[:, :, None], 0.0), axis=1)
        upper = amplitude.astype(jnp.bfloat16)
        lower = (amplitude - upper.astype(jnp.float32)).astype(jnp.bfloat16)
        total = total + jnp.dot(upper, table_block, preferred_element_type=jnp.float32)
        total = total + jnp.dot(lower, table_block, preferred_element_type=jnp.float32)
        return (total, None)

    empty = jnp.zeros((seg_index.shape[0], feature_count), jnp.float32)
    summed, unused = lax.scan(add_block, empty, (blocks, starts))
    return summed


def local(
    sent_act,
    sent_grad,
    stash_in,
    stash_pre,
    layer_weight,
    layer_bias,
    seg_table,
    seg_index,
    seg_amp,
    field_angle,
    angle_weight,
    target,
    sched,
):
    section_index = lax.axis_index("section")
    section_count = lax.axis_size("section")
    partial_value = lookup_sum(seg_table, seg_index, seg_amp, section_index * seg_table.shape[0])
    embedded = lax.psum(partial_value.astype(jnp.bfloat16), "section").astype(jnp.float32)
    angular = jnp.dot(field_angle, angle_weight, precision=lax.Precision.HIGHEST)
    first_input = (embedded + angular).astype(jnp.bfloat16)
    arrived = from_behind(sent_act[0], "section", 1)
    layer_input = jnp.where(section_index == 0, first_input, arrived)
    from_next = from_behind(sent_grad[0], "section", -1)
    stash_slot = sched[0]
    stashed_in = lax.dynamic_index_in_dim(stash_in[0], stash_slot, 0, keepdims=False)
    stashed_pre = lax.dynamic_index_in_dim(stash_pre[0], stash_slot, 0, keepdims=False)
    stashed_act, pullback = jax.vjp(jax.nn.gelu, stashed_pre.astype(jnp.float32))
    cotangent = jnp.where(
        section_index == section_count - 1,
        stashed_act - target.astype(jnp.float32),
        from_next.astype(jnp.float32),
    )
    pre_grad = pullback(cotangent)[0].astype(jnp.bfloat16)
    grad_bias = jnp.sum(pre_grad.astype(jnp.float32), axis=0)
    weight = layer_weight[0]
    pre_total = jnp.dot(
        lax.all_gather(layer_input, "fsdp", axis=1, tiled=True),
        weight,
        preferred_element_type=jnp.float32,
    )
    grad_total = lax.dot_general(
        lax.all_gather(stashed_in, "fsdp", axis=1, tiled=True),
        pre_grad,
        (((0,), (0,)), ((), ())),
        preferred_element_type=jnp.float32,
    )
    fwd_out = jax.nn.gelu(pre_total + layer_bias[0]).astype(jnp.bfloat16)
    partial_terms = lax.dot_general(
        pre_grad, weight, (((1,), (1,)), ((), ())), preferred_element_type=jnp.float32
    )
    grad_in = lax.psum_scatter(
        partial_terms.astype(jnp.bfloat16), "fsdp", scatter_dimension=1, tiled=True
    )
    return (fwd_out[None], grad_in[None], grad_total.astype(jnp.bfloat16)[None], grad_bias[None])


def solution(mesh):
    return jax.shard_map(
        local,
        mesh=mesh,
        in_specs=(
            P("section", "groups", "fsdp"),
            P("section", "groups", "fsdp"),
            P("section", None, "groups", "fsdp"),
            P("section", None, "groups", "fsdp"),
            P("section", None, "fsdp"),
            P("section", "fsdp"),
            P("section", "fsdp"),
            P("groups", None),
            P("groups", None),
            P("groups", None),
            P(None, "fsdp"),
            P("groups", "fsdp"),
            P("section"),
        ),
        out_specs=(
            P("section", "groups", "fsdp"),
            P("section", "groups", "fsdp"),
            P("section", "groups", "fsdp"),
            P("section", ("groups", "fsdp")),
        ),
        check_vma=False,
    )
```

profile of v0, /device:TPU:0, one launch (start us, length us, event | category | flops | bytes accessed | tf_op | source)
XLA Modules:
  0.0 238.5 jit_solution(12005963658422066757)
XLA Ops:
  10.9 3.7 %pad.4 = bf16[1536,1024]{1,0:T(8,128)(2,1)} pad(bf16[1196,1024]{1,0:T(8,128)(2,1)} %param.21, bf16[]{:T(256)} %constant.37.clone.1), padding=0_340x0_0 | pad | bytes 5595138 | tf_op jit(solution)/shard_map/jit(_pad)/pad | solution.py:18
  14.6 53.6 %while.11 = (s32[]{:T(128)}, f32[512,1024]{1,0:T(8,128)}, s32[512,32]{1,0:T(8,128)}, s32[3]{0:T(128)S(1)}, f32[512,32]{1,0:T(8,128)S(1)}, /*index=5*/bf16[3,512,1024]{2,1,0:T(8,128)(2,1)}, s32[]{:T(128)}, s32[]{:T(128)}) while((s32[]{:T(128)}, f32[512,1024]{1,0:T(8,128)}, s32[512,32]{1,0:T(8,128)}, s32[3]{0:T(128)S(1)}, ...), condition=%wide.region_2.3_spmd.clone, body=%wide.region_0.2_spmd.clone.sunk | while | flops 1101529600 | bytes 13766783 | solution.py:35
  15.8 9.0 %select_reduce_fusion.2 = f32[512,512]{1,0:T(8,128)S(1)} fusion(f32[512,32]{1,0:T(8,128)S(1)} %get-tuple-element.135, s32[512]{0:T(512)S(1)} %iota_add_fusion.2, s32[512,32]{1,0:T(8,128)} %get-tuple-element.133), kind=kLoop, calls=%fused_computation.clone.1 | loop fusion | flops 24903680 | bytes 1181696 | tf_op jit(solution)/shard_map/while/body/eval_jaxpr/reduce_sum | solution.py:27
  24.8 3.3 %fusion.57 = f32[512,1024]{1,0:T(8,128)} fusion(bf16[3,512,1024]{2,1,0:T(8,128)(2,1)} %get-tuple-element.136, s32[]{:T(128)S(6)} %copy.23, f32[512,512]{1,0:T(8,128)S(1)} %select_reduce_fusion.2), kind=kOutput, calls=%fused_computation.4.clone.1 | convolution fusion | flops 537133056 | bytes 4194308 | tf_op jit(solution)/shard_map/while/body/eval_jaxpr/dot_general | solution.py:30
  28.1 4.0 %fusion.58 = f32[512,1024]{1,0:T(8,128)} fusion(f32[512,1024]{1,0:T(8,128)} %fusion.57, f32[512,1024]{1,0:T(8,128)} %get-tuple-element.124, pred[]{:T(512)S(6)} %compare.4, bf16[3,512,1024]{2,1,0:T(8,128)(2,1)} %get-tuple-element.136, s32[]{:T(128)S(6)} %copy.23, f32[512,512]{1,0:T(8,128)S(1)} %select_reduce_fusion.2), kind=kOutput, calls=%fused_computation.2.clone.1 | convolution fusion | flops 539492352 | bytes 8388613 | tf_op jit(solution)/shard_map/while/body/eval_jaxpr/dot_general | solution.py:31
  33.3 9.0 %select_reduce_fusion.2 = f32[512,512]{1,0:T(8,128)S(1)} fusion(f32[512,32]{1,0:T(8,128)S(1)} %get-tuple-element.135, s32[512]{0:T(512)S(1)} %iota_add_fusion.2, s32[512,32]{1,0:T(8,128)} %get-tuple-element.133), kind=kLoop, calls=%fused_computation.clone.1 | loop fusion | flops 24903680 | bytes 1181696 | tf_op jit(solution)/shard_map/while/body/eval_jaxpr/reduce_sum | solution.py:27
  42.3 3.3 %fusion.57 = f32[512,1024]{1,0:T(8,128)} fusion(bf16[3,512,1024]{2,1,0:T(8,128)(2,1)} %get-tuple-element.136, s32[]{:T(128)S(6)} %copy.23, f32[512,512]{1,0:T(8,128)S(1)} %select_reduce_fusion.2), kind=kOutput, calls=%fused_computation.4.clone.1 | convolution fusion | flops 537133056 | bytes 4194308 | tf_op jit(solution)/shard_map/while/body/eval_jaxpr/dot_general | solution.py:30
  45.6 4.6 %fusion.58 = f32[512,1024]{1,0:T(8,128)} fusion(f32[512,1024]{1,0:T(8,128)} %fusion.57, f32[512,1024]{1,0:T(8,128)} %get-tuple-element.124, pred[]{:T(512)S(6)} %compare.4, bf16[3,512,1024]{2,1,0:T(8,128)(2,1)} %get-tuple-element.136, s32[]{:T(128)S(6)} %copy.23, f32[512,512]{1,0:T(8,128)S(1)} %select_reduce_fusion.2), kind=kOutput, calls=%fused_computation.2.clone.1 | convolution fusion | flops 539492352 | bytes 8388613 | tf_op jit(solution)/shard_map/while/body/eval_jaxpr/dot_general | solution.py:31
  51.4 9.0 %select_reduce_fusion.2 = f32[512,512]{1,0:T(8,128)S(1)} fusion(f32[512,32]{1,0:T(8,128)S(1)} %get-tuple-element.135, s32[512]{0:T(512)S(1)} %iota_add_fusion.2, s32[512,32]{1,0:T(8,128)} %get-tuple-element.133), kind=kLoop, calls=%fused_computation.clone.1 | loop fusion | flops 24903680 | bytes 1181696 | tf_op jit(solution)/shard_map/while/body/eval_jaxpr/reduce_sum | solution.py:27
  60.4 3.3 %fusion.57 = f32[512,1024]{1,0:T(8,128)} fusion(bf16[3,512,1024]{2,1,0:T(8,128)(2,1)} %get-tuple-element.136, s32[]{:T(128)S(6)} %copy.23, f32[512,512]{1,0:T(8,128)S(1)} %select_reduce_fusion.2), kind=kOutput, calls=%fused_computation.4.clone.1 | convolution fusion | flops 537133056 | bytes 4194308 | tf_op jit(solution)/shard_map/while/body/eval_jaxpr/dot_general | solution.py:30
  63.6 4.6 %fusion.58 = f32[512,1024]{1,0:T(8,128)} fusion(f32[512,1024]{1,0:T(8,128)} %fusion.57, f32[512,1024]{1,0:T(8,128)} %get-tuple-element.124, pred[]{:T(512)S(6)} %compare.4, bf16[3,512,1024]{2,1,0:T(8,128)(2,1)} %get-tuple-element.136, s32[]{:T(128)S(6)} %copy.23, f32[512,512]{1,0:T(8,128)S(1)} %select_reduce_fusion.2), kind=kOutput, calls=%fused_computation.2.clone.1 | convolution fusion | flops 539492352 | bytes 8388613 | tf_op jit(solution)/shard_map/while/body/eval_jaxpr/dot_general | solution.py:31
  68.2 2.7 %convert_element_type.47 = bf16[512,1024]{1,0:T(8,128)(2,1)} convert(f32[512,1024]{1,0:T(8,128)} %get-tuple-element.36) | non-fusion elementwise | flops 524288 | bytes 3145728 | tf_op jit(solution)/shard_map/convert_element_type | solution.py:57
  72.9 5.9 %collective-permute-start = (bf16[512,1024]{1,0:T(8,128)(2,1)}, bf16[512,1024]{1,0:T(8,128)(2,1)}, u32[]{:S(2)}, u32[]{:S(2)}) collective-permute-start(bf16[512,1024]{1,0:T(8,128)(2,1)} %bitcast.1), channel_id=1, source_target_pairs={{0,4},{4,8},{8,12},{1,5},{5,9},{9,13},{2,6},{6,10},{10,14},{3,7},{... | collective-permute-start | bytes 3145736 | tf_op jit(solution)/shard_map/ppermute | solution.py:10
  78.8 38.6 %collective-permute-done = bf16[512,1024]{1,0:T(8,128)(2,1)} collective-permute-done((bf16[512,1024]{1,0:T(8,128)(2,1)}, bf16[512,1024]{1,0:T(8,128)(2,1)}, u32[]{:S(2)}, u32[]{:S(2)}) %collective-permute-start) | collective-permute-done | bytes 1048608 | tf_op jit(solution)/shard_map/ppermute | solution.py:10
  117.4 23.2 %all-reduce.3.cloned.1.call-done = bf16[512,1024]{1,0:T(8,128)(2,1)} async-done(((bf16[512,1024]{1,0:T(8,128)(2,1)}), bf16[512,1024]{1,0:T(8,128)(2,1)}) %all-reduce.3.cloned.1.call-update) | async-done | bytes 1048592 | tf_op jit(solution)/shard_map/psum | solution.py:57
  140.7 4.2 %fusion.42 = bf16[512,1024]{1,0:T(8,128)(2,1)} fusion(bf16[512,1024]{1,0:T(8,128)(2,1)} %collective-permute-done, f32[512,2]{0,1:T(2,128)S(1)} %copy-done.5, f32[2,1024]{1,0:T(2,128)S(1)} %copy-done.4, bf16[512,1024]{1,0:T(8,128)(2,1)} %all-reduce.3.cloned.1.call-done, pred[]{:T(512)S(6)} %eq.19), kind=kOutput, calls=%fused_computation.49 | convolution fusion | flops 14680064 | bytes 3158017 | tf_op jit(solution)/shard_map/dot_general | solution.py:58
  144.9 1.5 collective-permute-start.1
  146.4 25.8 %collective-permute-done.1 = bf16[512,1024]{1,0:T(8,128)(2,1)} collective-permute-done((bf16[512,1024]{1,0:T(8,128)(2,1)}, bf16[512,1024]{1,0:T(8,128)(2,1)}, u32[]{:S(2)}, u32[]{:S(2)}) %collective-permute-start.1) | collective-permute-done | bytes 1048608 | tf_op jit(solution)/shard_map/ppermute | solution.py:10
  172.2 4.1 %convert_reduce_fusion = (f32[1024]{0:T(1024)}, bf16[512,1024]{1,0:T(8,128)(2,1)S(1)}) fusion(bf16[512,1024]{1,0:T(8,128)(2,1)} %collective-permute-done.1, bf16[512,1024]{1,0:T(8,128)(2,1)S(1)} %copy-done.1, bf16[1,2,512,1024]{3,2,1,0:T(8,128)(2,1)} %param.18, s32[]{:T(128)S(6)} %select_n.28, pred[]{:T(512)S(6)} %eq.20), kind=kLoop, calls=%fused_computation.46 | loop fusion | flops 14679040 | bytes 4198405 | tf_op jit(solution)/shard_map/reduce_sum | solution.py:73
  177.3 9.6 %fusion.14 = bf16[512,4096]{1,0:T(8,128)(2,1)} fusion(bf16[512,1024]{1,0:T(8,128)(2,1)S(1)} %get-tuple-element.77, bf16[1,4096,1024]{2,1,0:T(8,128)(2,1)} %param.19), kind=kOutput, calls=%fused_computation.19 | convolution fusion | flops 4297064448 | bytes 13631488 | tf_op jit(solution)/shard_map/dot_general | solution.py:87
  187.0 1.2 copy-done.3
  188.1 9.0 %convert_bitcast_fusion = bf16[1,4096,1024]{2,1,0:T(8,128)(2,1)} fusion(bf16[512,1024]{1,0:T(8,128)(2,1)S(1)} %copy-done.3, bf16[1,1,512,4096]{3,2,1,0:T(8,128)(2,1)} %all-gather.6.cloned.1.call-done), kind=kOutput, calls=%fused_computation.18 | convolution fusion | flops 4299161600 | bytes 13631488 | tf_op jit(solution)/shard_map/dot_general | solution.py:80
  197.1 10.7 %fusion.39 = bf16[1,512,1024]{2,1,0:T(8,128)(2,1)} fusion(bf16[512,4096]{1,0:T(8,128)(2,1)} %all-gather.4.cloned.1.call-done, bf16[1,4096,1024]{2,1,0:T(8,128)(2,1)} %param.19, f32[1024]{0:T(1024)S(1)} %bitcast.53), kind=kOutput, calls=%fused_computation.48 | convolution fusion | flops 4300210176 | bytes 13635584 | tf_op jit(solution)/shard_map/dot_general | solution.py:75
  207.8 23.1 %reduce-scatter.2.cloned.1.call-done = bf16[512,1024]{1,0:T(8,128)(2,1)} async-done(((bf16[512,4096]{1,0:T(8,128)(2,1)}), bf16[512,1024]{1,0:T(8,128)(2,1)}) %reduce-scatter.2.cloned.1.call-update) | async-done | bytes 1048592 | tf_op jit(solution)/shard_map/reduce_scatter | solution.py:90
  (35 shorter events, 8.9 us)
Async XLA Ops:
  8.0 63.7 %copy-start = (bf16[1,2,512,1024]{3,2,1,0:T(8,128)(2,1)S(1)}, bf16[1,2,512,1024]{3,2,1,0:T(8,128)(2,1)}, u32[]{:S(2)}) copy-start(bf16[1,2,512,1024]{3,2,1,0:T(8,128)(2,1)} %param.17) | copy-start | bytes 6291460
  8.0 132.6 %all-reduce.3.cloned.1.call-start = ((), (), s32[]{:S(2)}) async-start(), calls=%async_computation.1 | async-start | bytes 2097152 | tf_op jit(solution)/shard_map/psum | solution.py:57
  71.0 69.7 %copy-start.4 = (f32[2,1024]{1,0:T(2,128)S(1)}, f32[2,1024]{1,0:T(2,128)}, u32[]{:S(2)}) copy-start(f32[2,1024]{1,0:T(2,128)} %param.25) | copy-start | bytes 24580
  71.0 69.7 %copy-start.5 = (f32[512,2]{0,1:T(2,128)S(1)}, f32[512,2]{0,1:T(2,128)}, u32[]{:S(2)}) copy-start(f32[512,2]{0,1:T(2,128)} %param.24) | copy-start | bytes 12292
  71.0 116.0 %all-gather.6.cloned.1.call-start = ((), (), s32[]{:S(2)}) async-start(), calls=%async_computation.4 | async-start | bytes 5242880 | tf_op jit(solution)/shard_map/all_gather | solution.py:81
  72.9 124.2 %all-gather.4.cloned.1.call-start = ((), (), s32[]{:S(2)}) async-start(), calls=%async_computation.2 | async-start | bytes 5242880 | tf_op jit(solution)/shard_map/all_gather | solution.py:76
  72.9 44.5 %collective-permute-start = (bf16[512,1024]{1,0:T(8,128)(2,1)}, bf16[512,1024]{1,0:T(8,128)(2,1)}, u32[]{:S(2)}, u32[]{:S(2)}) collective-permute-start(bf16[512,1024]{1,0:T(8,128)(2,1)} %bitcast.1), channel_id=1, source_target_pairs={{0,4},{4,8},{8,12},{1,5},{5,9},{9,13},{2,6},{6,10},{10,14},{3,7},{... | collective-permute-start | bytes 3145736 | tf_op jit(solution)/shard_map/ppermute | solution.py:10
  78.8 93.4 %copy-start.1 = (bf16[512,1024]{1,0:T(8,128)(2,1)S(1)}, bf16[512,1024]{1,0:T(8,128)(2,1)}, u32[]{:S(2)}) copy-start(bf16[512,1024]{1,0:T(8,128)(2,1)} %param.26) | copy-start | bytes 3145732
  144.9 86.0 %reduce-scatter.2.cloned.1.call-start = ((), (), s32[]{:S(2)}) async-start(), calls=%async_computation.3 | async-start | bytes 5242880 | tf_op jit(solution)/shard_map/reduce_scatter | solution.py:90
  144.9 27.3 %collective-permute-start.1 = (bf16[512,1024]{1,0:T(8,128)(2,1)}, bf16[512,1024]{1,0:T(8,128)(2,1)}, u32[]{:S(2)}, u32[]{:S(2)}) collective-permute-start(bf16[512,1024]{1,0:T(8,128)(2,1)} %bitcast.51), channel_id=1, source_target_pairs={{4,0},{8,4},{12,8},{5,1},{9,5},{13,9},{6,2},{10,6},{14,10},{7,3},{... | collective-permute-start | bytes 3145736 | tf_op jit(solution)/shard_map/ppermute | solution.py:10
  176.3 1.0 copy-start.2
  186.9 1.2 copy-start.3
  186.9 10.2 %copy-start.6 = (f32[1,1024]{1,0:T(1,128)S(1)}, f32[1,1024]{1,0:T(1,128)}, u32[]{:S(2)}) copy-start(f32[1,1024]{1,0:T(1,128)} %param.20) | copy-start | bytes 12292
Sparse Core Ops, SparseCore 0:
  71.1 69.4 all-reduce.2
Sparse Core Ops, SparseCore 1:
  73.0 37.0 all-gather.5
  144.9 34.0 all-gather.3
  187.0 43.8 reduce-scatter.1
where the time goes:
time: 239 us; the launch traced here: 238 us
  waiting for transfers between devices  111 us (46%)
  matrix products  56.4 us (24%)
  other arithmetic  36.4 us (15%)
  between operations  16.4 us (7%)
  local copies, waits for them, and re-layouts  10.8 us (5%)
  starting transfers between devices  7.57 us (3%)
    ppermute x2, waiting for transfers between devices, from_behind(): return lax.ppermute(shard, axis, pairs)  64.4 us
    reduce_sum x3, other arithmetic, add_block(): amplitude = jnp.sum(jnp.where(matched, seg_amp[:, :, None], 0.0), axis=1)  26.9 us
    psum x1, waiting for transfers between devices, local(): lax.psum(partial_value.astype(jnp.bfloat16), 'section').astype(jnp.float32)  23.2 us
    reduce_scatter x1, waiting for transfers between devices, local(): lax.psum_scatter(partial_terms.astype(jnp.bfloat16), 'fsdp', scatter_dime...  23.1 us
    dot_general x3, matrix products, add_block(): jnp.dot(lower, table_block, preferred_element_type=jnp.float32)  13.2 us
    dot_general x1, matrix products, local(): jnp.dot(lax.all_gather(layer_input, 'fsdp', axis=1, tiled=True), weight,...  10.7 us
    dot_general x3, matrix products, add_block(): jnp.dot(upper, table_block, preferred_element_type=jnp.float32)  9.82 us
    dot_general x1, matrix products, local(): lax.dot_general(pre_grad, weight, (((1,), (1,)), ((), ())), preferred_ele...  9.61 us
  transfers between devices with their start and end apart: 6, of which 4 were waited for; matrix products, arithmetic and copies ran while one was open for 16% of the time, Pallas kernels for 0%

commit v1 on v0

--- a/solution.py
+++ b/solution.py
@@ -54,7 +54,9 @@
     section_index = lax.axis_index("section")
     section_count = lax.axis_size("section")
     partial_value = lookup_sum(seg_table, seg_index, seg_amp, section_index * seg_table.shape[0])
-    embedded = lax.psum(partial_value.astype(jnp.bfloat16), "section").astype(jnp.float32)
+    embedded = jnp.sum(
+        lax.all_gather(partial_value.astype(jnp.bfloat16), "section"), axis=0
+    ).astype(jnp.float32)
     angular = jnp.dot(field_angle, angle_weight, precision=lax.Precision.HIGHEST)
     first_input = (embedded + angular).astype(jnp.bfloat16)
     arrived = from_behind(sent_act[0], "section", 1)

time: 239 us -> 298 us (1.25)
  waiting for transfers between devices: 111 us -> 171 us
  other arithmetic: 36.4 us -> 40 us
    all_gather x0 -> x1, waiting for transfers between devices: none -> 89.4 us  [local(): lax.all_gather(partial_value.astype(jnp.bfloat16), 'section')]
    ppermute x2, waiting for transfers between devices: 64.4 us -> 28 us  [from_behind(): return lax.ppermute(shard, axis, pairs)]
    psum x1 -> x0, waiting for transfers between devices: 23.2 us -> none  [local(): lax.psum(partial_value.astype(jnp.bfloat16), 'section').astype(jnp.float32)]
    all_gather x1, waiting for transfers between devices: 0.01 us -> 16.4 us  [local(): lax.all_gather(layer_input, 'fsdp', axis=1, tiled=True)]
    reduce_scatter x1, waiting for transfers between devices: 23.1 us -> 36.9 us  [local(): lax.psum_scatter(partial_terms.astype(jnp.bfloat16), 'fsdp', scatter_dime...]
    reduce_sum x0 -> x1, other arithmetic: none -> 3.35 us  [local(): jnp.sum(lax.all_gather(partial_value.astype(jnp.bfloat16), 'section'), ax...]
  transfers between devices with their start and end apart: 6 -> 6, of which waited for: 4 -> 4; matrix products, arithmetic and copies ran while one was open for 16% -> 14% of each run, Pallas kernels for 0% -> 0%
where the time goes in v1:
time: 298 us; the launch traced here: 297 us
  waiting for transfers between devices  171 us (57%)
  matrix products  55.1 us (18%)
  other arithmetic  40 us (13%)
  between operations  14.5 us (5%)
  local copies, waits for them, and re-layouts  8.59 us (3%)
  starting transfers between devices  7.63 us (3%)
    all_gather x1, waiting for transfers between devices, local(): lax.all_gather(partial_value.astype(jnp.bfloat16), 'section')  89.4 us
    reduce_scatter x1, waiting for transfers between devices, local(): lax.psum_scatter(partial_terms.astype(jnp.bfloat16), 'fsdp', scatter_dime...  36.9 us
    ppermute x2, waiting for transfers between devices, from_behind(): return lax.ppermute(shard, axis, pairs)  28 us
    reduce_sum x3, other arithmetic, add_block(): amplitude = jnp.sum(jnp.where(matched, seg_amp[:, :, None], 0.0), axis=1)  26.9 us
    all_gather x1, waiting for transfers between devices, local(): lax.all_gather(layer_input, 'fsdp', axis=1, tiled=True)  16.4 us
    dot_general x3, matrix products, add_block(): jnp.dot(lower, table_block, preferred_element_type=jnp.float32)  13.1 us
    dot_general x1, matrix products, local(): jnp.dot(lax.all_gather(layer_input, 'fsdp', axis=1, tiled=True), weight,...  10.6 us
    dot_general x3, matrix products, add_block(): jnp.dot(upper, table_block, preferred_element_type=jnp.float32)  9.87 us
  transfers between devices with their start and end apart: 6, of which 4 were waited for; matrix products, arithmetic and copies ran while one was open for 14% of the time, Pallas kernels for 0%

profile of v1, /device:TPU:0, one launch (start us, length us, event | category | flops | bytes accessed | tf_op | source)
XLA Modules:
  0.0 296.8 jit_solution(17201320122542406387)
XLA Ops:
  10.1 3.7 %pad.4 = bf16[1536,1024]{1,0:T(8,128)(2,1)} pad(bf16[1196,1024]{1,0:T(8,128)(2,1)} %param.21, bf16[]{:T(256)} %constant.38.clone.1), padding=0_340x0_0 | pad | bytes 5595138 | tf_op jit(solution)/shard_map/jit(_pad)/pad | solution.py:18
  13.8 53.6 %while.11 = (s32[]{:T(128)}, f32[512,1024]{1,0:T(8,128)}, s32[512,32]{1,0:T(8,128)}, s32[3]{0:T(128)S(1)}, f32[512,32]{1,0:T(8,128)S(1)}, /*index=5*/bf16[3,512,1024]{2,1,0:T(8,128)(2,1)}, s32[]{:T(128)}, s32[]{:T(128)}) while((s32[]{:T(128)}, f32[512,1024]{1,0:T(8,128)}, s32[512,32]{1,0:T(8,128)}, s32[3]{0:T(128)S(1)}, ...), condition=%wide.region_2.3_spmd.clone, body=%wide.region_0.2_spmd.clone.sunk | while | flops 1101529600 | bytes 13766783 | solution.py:35
  15.0 9.0 %select_reduce_fusion.2 = f32[512,512]{1,0:T(8,128)S(1)} fusion(f32[512,32]{1,0:T(8,128)S(1)} %get-tuple-element.135, s32[512]{0:T(512)S(1)} %iota_add_fusion.2, s32[512,32]{1,0:T(8,128)} %get-tuple-element.133), kind=kLoop, calls=%fused_computation.clone.1 | loop fusion | flops 24903680 | bytes 1181696 | tf_op jit(solution)/shard_map/while/body/eval_jaxpr/reduce_sum | solution.py:27
  24.0 3.3 %fusion.57 = f32[512,1024]{1,0:T(8,128)} fusion(bf16[3,512,1024]{2,1,0:T(8,128)(2,1)} %get-tuple-element.136, s32[]{:T(128)S(6)} %copy.23, f32[512,512]{1,0:T(8,128)S(1)} %select_reduce_fusion.2), kind=kOutput, calls=%fused_computation.4.clone.1 | convolution fusion | flops 537133056 | bytes 4194308 | tf_op jit(solution)/shard_map/while/body/eval_jaxpr/dot_general | solution.py:30
  27.3 3.9 %fusion.58 = f32[512,1024]{1,0:T(8,128)} fusion(f32[512,1024]{1,0:T(8,128)} %fusion.57, f32[512,1024]{1,0:T(8,128)} %get-tuple-element.124, pred[]{:T(512)S(6)} %compare.4, bf16[3,512,1024]{2,1,0:T(8,128)(2,1)} %get-tuple-element.136, s32[]{:T(128)S(6)} %copy.23, f32[512,512]{1,0:T(8,128)S(1)} %select_reduce_fusion.2), kind=kOutput, calls=%fused_computation.2.clone.1 | convolution fusion | flops 539492352 | bytes 8388613 | tf_op jit(solution)/shard_map/while/body/eval_jaxpr/dot_general | solution.py:31
  32.5 9.0 %select_reduce_fusion.2 = f32[512,512]{1,0:T(8,128)S(1)} fusion(f32[512,32]{1,0:T(8,128)S(1)} %get-tuple-element.135, s32[512]{0:T(512)S(1)} %iota_add_fusion.2, s32[512,32]{1,0:T(8,128)} %get-tuple-element.133), kind=kLoop, calls=%fused_computation.clone.1 | loop fusion | flops 24903680 | bytes 1181696 | tf_op jit(solution)/shard_map/while/body/eval_jaxpr/reduce_sum | solution.py:27
  41.4 3.3 %fusion.57 = f32[512,1024]{1,0:T(8,128)} fusion(bf16[3,512,1024]{2,1,0:T(8,128)(2,1)} %get-tuple-element.136, s32[]{:T(128)S(6)} %copy.23, f32[512,512]{1,0:T(8,128)S(1)} %select_reduce_fusion.2), kind=kOutput, calls=%fused_computation.4.clone.1 | convolution fusion | flops 537133056 | bytes 4194308 | tf_op jit(solution)/shard_map/while/body/eval_jaxpr/dot_general | solution.py:30
  44.7 4.6 %fusion.58 = f32[512,1024]{1,0:T(8,128)} fusion(f32[512,1024]{1,0:T(8,128)} %fusion.57, f32[512,1024]{1,0:T(8,128)} %get-tuple-element.124, pred[]{:T(512)S(6)} %compare.4, bf16[3,512,1024]{2,1,0:T(8,128)(2,1)} %get-tuple-element.136, s32[]{:T(128)S(6)} %copy.23, f32[512,512]{1,0:T(8,128)S(1)} %select_reduce_fusion.2), kind=kOutput, calls=%fused_computation.2.clone.1 | convolution fusion | flops 539492352 | bytes 8388613 | tf_op jit(solution)/shard_map/while/body/eval_jaxpr/dot_general | solution.py:31
  50.6 9.0 %select_reduce_fusion.2 = f32[512,512]{1,0:T(8,128)S(1)} fusion(f32[512,32]{1,0:T(8,128)S(1)} %get-tuple-element.135, s32[512]{0:T(512)S(1)} %iota_add_fusion.2, s32[512,32]{1,0:T(8,128)} %get-tuple-element.133), kind=kLoop, calls=%fused_computation.clone.1 | loop fusion | flops 24903680 | bytes 1181696 | tf_op jit(solution)/shard_map/while/body/eval_jaxpr/reduce_sum | solution.py:27
  59.5 3.3 %fusion.57 = f32[512,1024]{1,0:T(8,128)} fusion(bf16[3,512,1024]{2,1,0:T(8,128)(2,1)} %get-tuple-element.136, s32[]{:T(128)S(6)} %copy.23, f32[512,512]{1,0:T(8,128)S(1)} %select_reduce_fusion.2), kind=kOutput, calls=%fused_computation.4.clone.1 | convolution fusion | flops 537133056 | bytes 4194308 | tf_op jit(solution)/shard_map/while/body/eval_jaxpr/dot_general | solution.py:30
  62.8 4.6 %fusion.58 = f32[512,1024]{1,0:T(8,128)} fusion(f32[512,1024]{1,0:T(8,128)} %fusion.57, f32[512,1024]{1,0:T(8,128)} %get-tuple-element.124, pred[]{:T(512)S(6)} %compare.4, bf16[3,512,1024]{2,1,0:T(8,128)(2,1)} %get-tuple-element.136, s32[]{:T(128)S(6)} %copy.23, f32[512,512]{1,0:T(8,128)S(1)} %select_reduce_fusion.2), kind=kOutput, calls=%fused_computation.2.clone.1 | convolution fusion | flops 539492352 | bytes 8388613 | tf_op jit(solution)/shard_map/while/body/eval_jaxpr/dot_general | solution.py:31
  67.4 2.7 convert_element_type.49
  72.0 6.0 %collective-permute-start = (bf16[512,1024]{1,0:T(8,128)(2,1)}, bf16[512,1024]{1,0:T(8,128)(2,1)}, u32[]{:S(2)}, u32[]{:S(2)}) collective-permute-start(bf16[512,1024]{1,0:T(8,128)(2,1)} %bitcast.2), channel_id=1, source_target_pairs={{0,4},{4,8},{8,12},{1,5},{5,9},{9,13},{2,6},{6,10},{10,14},{3,7},{... | collective-permute-start | bytes 3145736 | tf_op jit(solution)/shard_map/ppermute | solution.py:10
  78.0 89.4 %all-gather.8.cloned.1.call-done = bf16[2048,1024]{1,0:T(8,128)(2,1)} async-done(((bf16[512,1024]{1,0:T(8,128)(2,1)}), bf16[2048,1024]{1,0:T(8,128)(2,1)}) %all-gather.8.cloned.1.call-update) | async-done | bytes 4194320 | tf_op jit(solution)/shard_map/all_gather | solution.py:58
  167.4 3.3 %reduce_sum.30 = bf16[512,1024]{1,0:T(8,128)(2,1)S(1)} reduce(bf16[4,512,1024]{2,1,0:T(8,128)(2,1)} %bitcast.51, bf16[]{:T(256)} %constant.38.clone.1), dimensions={0}, to_apply=%region_3.4 | reduce | flops 1572864 | bytes 5242882 | tf_op jit(solution)/shard_map/reduce_sum | solution.py:57
  170.8 3.0 %fusion.42 = bf16[512,1024]{1,0:T(8,128)(2,1)} fusion(bf16[512,1024]{1,0:T(8,128)(2,1)} %collective-permute-done, f32[512,2]{0,1:T(2,128)S(1)} %copy-done.2, f32[2,1024]{1,0:T(2,128)S(1)} %copy-done.1, bf16[512,1024]{1,0:T(8,128)(2,1)S(1)} %reduce_sum.30, pred[]{:T(512)S(6)} %eq.19), kind=kOutput, calls=%fused_computation.49 | convolution fusion | flops 14680064 | bytes 3158017 | tf_op jit(solution)/shard_map/dot_general | solution.py:60
  173.9 1.5 collective-permute-start.1
  175.4 28.0 %collective-permute-done.1 = bf16[512,1024]{1,0:T(8,128)(2,1)} collective-permute-done((bf16[512,1024]{1,0:T(8,128)(2,1)}, bf16[512,1024]{1,0:T(8,128)(2,1)}, u32[]{:S(2)}, u32[]{:S(2)}) %collective-permute-start.1) | collective-permute-done | bytes 1048608 | tf_op jit(solution)/shard_map/ppermute | solution.py:10
  203.4 4.3 %convert_reduce_fusion = (f32[1024]{0:T(1024)}, bf16[512,1024]{1,0:T(8,128)(2,1)S(1)}) fusion(bf16[512,1024]{1,0:T(8,128)(2,1)} %collective-permute-done.1, bf16[512,1024]{1,0:T(8,128)(2,1)} %param.26, bf16[1,2,512,1024]{3,2,1,0:T(8,128)(2,1)} %param.18, s32[]{:T(128)S(6)} %select_n.28, pred[]{:T(512)S(6)} %eq.20), kind=kLoop, calls=%fused_computation.46 | loop fusion | flops 14679040 | bytes 4198405 | tf_op jit(solution)/shard_map/reduce_sum | solution.py:75
  207.7 9.5 %fusion.14 = bf16[512,4096]{1,0:T(8,128)(2,1)} fusion(bf16[512,1024]{1,0:T(8,128)(2,1)S(1)} %get-tuple-element.77, bf16[1,4096,1024]{2,1,0:T(8,128)(2,1)} %param.19), kind=kOutput, calls=%fused_computation.19 | convolution fusion | flops 4297064448 | bytes 13631488 | tf_op jit(solution)/shard_map/dot_general | solution.py:89
  217.3 9.1 %convert_bitcast_fusion = bf16[1,4096,1024]{2,1,0:T(8,128)(2,1)} fusion(bf16[512,1024]{1,0:T(8,128)(2,1)S(1)} %get-tuple-element.77, bf16[1,1,512,4096]{3,2,1,0:T(8,128)(2,1)} %all-gather.10.cloned.1.call-done), kind=kOutput, calls=%fused_computation.18 | convolution fusion | flops 4299161600 | bytes 13631488 | tf_op jit(solution)/shard_map/dot_general | solution.py:82
  226.4 16.4 %all-gather.6.cloned.1.call-done = bf16[512,4096]{1,0:T(8,128)(2,1)} async-done(((bf16[512,1024]{1,0:T(8,128)(2,1)}), bf16[512,4096]{1,0:T(8,128)(2,1)}) %all-gather.6.cloned.1.call-update) | async-done | bytes 4194320 | tf_op jit(solution)/shard_map/all_gather | solution.py:78
  242.8 10.6 %fusion.39 = bf16[1,512,1024]{2,1,0:T(8,128)(2,1)} fusion(bf16[512,4096]{1,0:T(8,128)(2,1)} %all-gather.6.cloned.1.call-done, bf16[1,4096,1024]{2,1,0:T(8,128)(2,1)} %param.19, f32[1024]{0:T(1024)S(1)} %bitcast.55), kind=kOutput, calls=%fused_computation.48 | convolution fusion | flops 4300210176 | bytes 13635584 | tf_op jit(solution)/shard_map/dot_general | solution.py:77
  253.4 36.9 %reduce-scatter.2.cloned.1.call-done = bf16[512,1024]{1,0:T(8,128)(2,1)} async-done(((bf16[512,4096]{1,0:T(8,128)(2,1)}), bf16[512,1024]{1,0:T(8,128)(2,1)}) %reduce-scatter.2.cloned.1.call-update) | async-done | bytes 1048592 | tf_op jit(solution)/shard_map/reduce_scatter | solution.py:92
  (30 shorter events, 7.8 us)
Async XLA Ops:
  7.2 63.7 %copy-start = (bf16[1,2,512,1024]{3,2,1,0:T(8,128)(2,1)S(1)}, bf16[1,2,512,1024]{3,2,1,0:T(8,128)(2,1)}, u32[]{:S(2)}) copy-start(bf16[1,2,512,1024]{3,2,1,0:T(8,128)(2,1)} %param.17) | copy-start | bytes 6291460
  7.2 160.3 %all-gather.8.cloned.1.call-start = ((), (), s32[]{:S(2)}) async-start(), calls=%async_computation.3 | async-start | bytes 5242880 | tf_op jit(solution)/shard_map/all_gather | solution.py:58
  70.2 147.1 %all-gather.10.cloned.1.call-start = ((), (), s32[]{:S(2)}) async-start(), calls=%async_computation.4 | async-start | bytes 5242880 | tf_op jit(solution)/shard_map/all_gather | solution.py:83
  71.9 170.9 %all-gather.6.cloned.1.call-start = ((), (), s32[]{:S(2)}) async-start(), calls=%async_computation.1 | async-start | bytes 5242880 | tf_op jit(solution)/shard_map/all_gather | solution.py:78
  72.0 98.8 %collective-permute-start = (bf16[512,1024]{1,0:T(8,128)(2,1)}, bf16[512,1024]{1,0:T(8,128)(2,1)}, u32[]{:S(2)}, u32[]{:S(2)}) collective-permute-start(bf16[512,1024]{1,0:T(8,128)(2,1)} %bitcast.2), channel_id=1, source_target_pairs={{0,4},{4,8},{8,12},{1,5},{5,9},{9,13},{2,6},{6,10},{10,14},{3,7},{... | collective-permute-start | bytes 3145736 | tf_op jit(solution)/shard_map/ppermute | solution.py:10
  167.4 3.4 %copy-start.1 = (f32[2,1024]{1,0:T(2,128)S(1)}, f32[2,1024]{1,0:T(2,128)}, u32[]{:S(2)}) copy-start(f32[2,1024]{1,0:T(2,128)} %param.25) | copy-start | bytes 24580
  167.4 3.4 %copy-start.2 = (f32[512,2]{0,1:T(2,128)S(1)}, f32[512,2]{0,1:T(2,128)}, u32[]{:S(2)}) copy-start(f32[512,2]{0,1:T(2,128)} %param.24) | copy-start | bytes 12292
  173.8 116.5 %reduce-scatter.2.cloned.1.call-start = ((), (), s32[]{:S(2)}) async-start(), calls=%async_computation.2 | async-start | bytes 5242880 | tf_op jit(solution)/shard_map/reduce_scatter | solution.py:92
  173.9 29.5 %collective-permute-start.1 = (bf16[512,1024]{1,0:T(8,128)(2,1)}, bf16[512,1024]{1,0:T(8,128)(2,1)}, u32[]{:S(2)}, u32[]{:S(2)}) collective-permute-start(bf16[512,1024]{1,0:T(8,128)(2,1)} %bitcast.53), channel_id=1, source_target_pairs={{4,0},{8,4},{12,8},{5,1},{9,5},{13,9},{6,2},{10,6},{14,10},{7,3},{... | collective-permute-start | bytes 3145736 | tf_op jit(solution)/shard_map/ppermute | solution.py:10
  217.2 25.6 %copy-start.3 = (f32[1,1024]{1,0:T(1,128)S(1)}, f32[1,1024]{1,0:T(1,128)}, u32[]{:S(2)}) copy-start(f32[1,1024]{1,0:T(1,128)} %param.20) | copy-start | bytes 12292
Sparse Core Ops, SparseCore 0:
  70.3 97.1 all-gather.7
  169.6 36.5 all-gather.9
  208.3 34.4 all-gather.5
  245.8 44.4 reduce-scatter.1
